TPU v7x, 32 devices: a whole 2x2x4 slice. The times are simulated.
32 devices in a mesh: groups: 2 (over y), dp: 4 (over z), feat: 2 (over x), node: 2 (over core).
Axes of the slice: x: 2, y: 2, z: 4, core: 2. Of those that a mesh axis runs over, the one named last changes fastest.
Arguments:
- bins: int32 [256, 32768], P('feat', ('groups', 'dp')), parts along dimension 1, may hold values from 0 to 255
- node_ids: int32 [32768], P(('groups', 'dp')), parts along dimension 0, may hold values from 0 to 63
- grad: bfloat16 [32768], P(('groups', 'dp')), parts along dimension 0, may hold values from -1 to 1
- hess: bfloat16 [32768], P(('groups', 'dp')), parts along dimension 0, may hold values from 0.019897461 to 0.25
Outputs:
- gains: float32 [128, 256, 256], P(('groups', 'node'), ('feat', 'dp')), parts along dimension 0
- best: float32 [128], P(('groups', 'node')), parts along dimension 0
There are 2 independent parts, one for each index of `groups`. A program takes and returns all parts, laid end to end along the dimension named above; each array names one. Nothing has to cross between parts.
All inputs are finite; a program needn't handle non-finite values.
Results may differ from a plain program's by a relative error of at most 0.0003.
Values sent between devices are 32-bit elements; how exact they have to be, the bound alone decides.
A program may use at most 64 MiB of HBM per device.

v0:
```python
import math

import jax
import jax.numpy as jnp
from jax import lax
from jax.sharding import PartitionSpec as P

BINS = 256
NODES = 64


LAMBDA_REG = 1.0


def histogram(bin_table, weights, feature_amount):
    block_size = math.gcd(feature_amount, 8)
    levels = jnp.arange(BINS, dtype=jnp.int32)
    width = weights.shape[1]

    def one_block(position):
        columns = lax.dynamic_slice_in_dim(bin_table, position * block_size, block_size, 0)
        onehot = (columns[:, :, None] == levels).astype(jnp.bfloat16)
        return jnp.einsum("frb,rk->fbk", onehot, weights, preferred_element_type=jnp.float32)

    blocks_out = lax.map(one_block, jnp.arange(feature_amount // block_size, dtype=jnp.int32))
    return blocks_out.reshape(feature_amount, BINS, width)


def on_device(bins, node_ids, grad, hess):
    feature_block, row_count = bins.shape
    node_count = NODES // lax.axis_size("node")
    node_base = lax.axis_index("node") * node_count
    own_features = feature_block // lax.axis_size("dp")
    own_nodes = (node_ids[:, None] == node_base + jnp.arange(node_count, dtype=jnp.int32)).astype(
        jnp.bfloat16
    )
    weights = jnp.stack([own_nodes * grad[:, None], own_nodes * hess[:, None]], 2).reshape(
        row_count, node_count * 2
    )
    summed = lax.psum_scatter(
        histogram(bins, weights, lax.axis_size("dp") * own_features),
        "dp",
        scatter_dimension=0,
        tiled=True,
    )
    hist = jnp.transpose(summed.reshape(own_features, BINS, node_count, 2), (2, 0, 1, 3))
    own_float = (node_ids[:, None] == node_base + jnp.arange(node_count, dtype=jnp.int32)).astype(
        jnp.float32
    )
    stats = jnp.stack([grad.astype(jnp.float32), hess.astype(jnp.float32)], 1)
    local_totals = jnp.einsum("rn,rs->ns", own_float, stats, precision=lax.Precision.HIGHEST)
    totals = lax.psum(local_totals, "dp")
    cumulated = jnp.cumsum(hist, axis=2)
    grad_left = cumulated[..., 0]
    hess_left = cumulated[..., 1]
    grad_total = totals[:, 0][:, None, None]
    hess_total = totals[:, 1][:, None, None]
    gains = 0.5 * (
        grad_left * grad_left / (hess_left + LAMBDA_REG)
        + (grad_total - grad_left) ** 2 / (hess_total - hess_left + LAMBDA_REG)
        - grad_total * grad_total / (hess_total + LAMBDA_REG)
    )
    best = lax.pmax(jnp.max(gains, axis=(1, 2)), ("dp", "feat"))
    return (gains, best)


def solution(mesh):
    return jax.shard_map(
        on_device,
        mesh=mesh,
        in_specs=(
            P("feat", ("groups", "dp")),
            P(("groups", "dp")),
            P(("groups", "dp")),
            P(("groups", "dp")),
        ),
        out_specs=(P(("groups", "node"), ("feat", "dp"), None), P(("groups", "node"))),
        check_vma=False,
    )
```

profile of v0, /device:TPU:0, one launch (start us, length us, event | category | flops | bytes accessed | tf_op | source)
XLA Modules:
  0.0 417.4 jit_solution(2708311447517929196)
XLA Ops:
  7.2 1.9 compare_select_fusion.1
  9.1 1.2 pad_maximum_fusion
  10.3 0.2 reshape.182
  10.6 155.4 %while.11 = (s32[]{:T(128)}, f32[16,8,256,64]{2,3,1,0:T(8,128)}, s32[16]{0:T(128)S(1)}, s32[128,4096]{1,0:T(8,128)}, bf16[4096,64]{0,1:T(8,128)(2,1)S(1)}, /*index=5*/s32[]{:T(128)}, s32[1]{0:T(128)}, s32[]{:T(128)}, s32[]{:T(128)}) while((s32[]{:T(128)}, f32[16,8,256,64]{2,3,1,0:T(8,128)}, s32[16]{0:T(128)S(1)}, ...), condition=%wide.region_1.2_spmd.clone, body=%wide.region_0.1_spmd.clone.sunk | while | flops 1082130432 | bytes 1442459 | solution.py:25
  10.6 0.6 dynamic_slice.13
  11.8 0.9 constant_dynamic-slice_fusion.2
  12.7 7.5 %fusion.19 = f32[16,8,256,64]{2,3,1,0:T(8,128)} fusion(f32[16,8,256,64]{2,3,1,0:T(8,128)} %get-tuple-element.104, s32[]{:T(128)} %get-tuple-element.103, s32[8,4096]{1,0:T(8,128)S(1)} %constant_dynamic-slice_fusion.2, bf16[4096,64]{0,1:T(8,128)(2,1)S(1)} %get-tuple-element.116), kind=kOutput, calls=%fused_computation.5.clone.1 | convolution fusion | flops 1082130432 | bytes 1180160 | tf_op jit(solution)/shard_map/while/body/eval_jaxpr/frb,rk->fbk/dot_general | solution.py:23
  20.3 0.6 dynamic_slice.13
  21.5 0.9 constant_dynamic-slice_fusion.2
  22.4 7.6 %fusion.19 = f32[16,8,256,64]{2,3,1,0:T(8,128)} fusion(f32[16,8,256,64]{2,3,1,0:T(8,128)} %get-tuple-element.104, s32[]{:T(128)} %get-tuple-element.103, s32[8,4096]{1,0:T(8,128)S(1)} %constant_dynamic-slice_fusion.2, bf16[4096,64]{0,1:T(8,128)(2,1)S(1)} %get-tuple-element.116), kind=kOutput, calls=%fused_computation.5.clone.1 | convolution fusion | flops 1082130432 | bytes 1180160 | tf_op jit(solution)/shard_map/while/body/eval_jaxpr/frb,rk->fbk/dot_general | solution.py:23
  30.0 0.6 dynamic_slice.13
  31.2 0.9 constant_dynamic-slice_fusion.2
  32.2 7.5 %fusion.19 = f32[16,8,256,64]{2,3,1,0:T(8,128)} fusion(f32[16,8,256,64]{2,3,1,0:T(8,128)} %get-tuple-element.104, s32[]{:T(128)} %get-tuple-element.103, s32[8,4096]{1,0:T(8,128)S(1)} %constant_dynamic-slice_fusion.2, bf16[4096,64]{0,1:T(8,128)(2,1)S(1)} %get-tuple-element.116), kind=kOutput, calls=%fused_computation.5.clone.1 | convolution fusion | flops 1082130432 | bytes 1180160 | tf_op jit(solution)/shard_map/while/body/eval_jaxpr/frb,rk->fbk/dot_general | solution.py:23
  39.7 0.6 dynamic_slice.13
  41.0 0.9 constant_dynamic-slice_fusion.2
  41.9 7.5 %fusion.19 = f32[16,8,256,64]{2,3,1,0:T(8,128)} fusion(f32[16,8,256,64]{2,3,1,0:T(8,128)} %get-tuple-element.104, s32[]{:T(128)} %get-tuple-element.103, s32[8,4096]{1,0:T(8,128)S(1)} %constant_dynamic-slice_fusion.2, bf16[4096,64]{0,1:T(8,128)(2,1)S(1)} %get-tuple-element.116), kind=kOutput, calls=%fused_computation.5.clone.1 | convolution fusion | flops 1082130432 | bytes 1180160 | tf_op jit(solution)/shard_map/while/body/eval_jaxpr/frb,rk->fbk/dot_general | solution.py:23
  49.4 0.6 dynamic_slice.13
  50.7 0.9 constant_dynamic-slice_fusion.2
  51.6 7.5 %fusion.19 = f32[16,8,256,64]{2,3,1,0:T(8,128)} fusion(f32[16,8,256,64]{2,3,1,0:T(8,128)} %get-tuple-element.104, s32[]{:T(128)} %get-tuple-element.103, s32[8,4096]{1,0:T(8,128)S(1)} %constant_dynamic-slice_fusion.2, bf16[4096,64]{0,1:T(8,128)(2,1)S(1)} %get-tuple-element.116), kind=kOutput, calls=%fused_computation.5.clone.1 | convolution fusion | flops 1082130432 | bytes 1180160 | tf_op jit(solution)/shard_map/while/body/eval_jaxpr/frb,rk->fbk/dot_general | solution.py:23
  59.1 0.6 dynamic_slice.13
  60.4 0.9 constant_dynamic-slice_fusion.2
  61.3 7.5 %fusion.19 = f32[16,8,256,64]{2,3,1,0:T(8,128)} fusion(f32[16,8,256,64]{2,3,1,0:T(8,128)} %get-tuple-element.104, s32[]{:T(128)} %get-tuple-element.103, s32[8,4096]{1,0:T(8,128)S(1)} %constant_dynamic-slice_fusion.2, bf16[4096,64]{0,1:T(8,128)(2,1)S(1)} %get-tuple-element.116), kind=kOutput, calls=%fused_computation.5.clone.1 | convolution fusion | flops 1082130432 | bytes 1180160 | tf_op jit(solution)/shard_map/while/body/eval_jaxpr/frb,rk->fbk/dot_general | solution.py:23
  68.8 0.6 dynamic_slice.13
  70.1 0.9 constant_dynamic-slice_fusion.2
  71.0 7.5 %fusion.19 = f32[16,8,256,64]{2,3,1,0:T(8,128)} fusion(f32[16,8,256,64]{2,3,1,0:T(8,128)} %get-tuple-element.104, s32[]{:T(128)} %get-tuple-element.103, s32[8,4096]{1,0:T(8,128)S(1)} %constant_dynamic-slice_fusion.2, bf16[4096,64]{0,1:T(8,128)(2,1)S(1)} %get-tuple-element.116), kind=kOutput, calls=%fused_computation.5.clone.1 | convolution fusion | flops 1082130432 | bytes 1180160 | tf_op jit(solution)/shard_map/while/body/eval_jaxpr/frb,rk->fbk/dot_general | solution.py:23
  78.6 0.6 dynamic_slice.13
  79.8 0.9 constant_dynamic-slice_fusion.2
  80.7 7.5 %fusion.19 = f32[16,8,256,64]{2,3,1,0:T(8,128)} fusion(f32[16,8,256,64]{2,3,1,0:T(8,128)} %get-tuple-element.104, s32[]{:T(128)} %get-tuple-element.103, s32[8,4096]{1,0:T(8,128)S(1)} %constant_dynamic-slice_fusion.2, bf16[4096,64]{0,1:T(8,128)(2,1)S(1)} %get-tuple-element.116), kind=kOutput, calls=%fused_computation.5.clone.1 | convolution fusion | flops 1082130432 | bytes 1180160 | tf_op jit(solution)/shard_map/while/body/eval_jaxpr/frb,rk->fbk/dot_general | solution.py:23
  88.3 0.6 dynamic_slice.13
  89.5 0.9 constant_dynamic-slice_fusion.2
  90.4 7.5 %fusion.19 = f32[16,8,256,64]{2,3,1,0:T(8,128)} fusion(f32[16,8,256,64]{2,3,1,0:T(8,128)} %get-tuple-element.104, s32[]{:T(128)} %get-tuple-element.103, s32[8,4096]{1,0:T(8,128)S(1)} %constant_dynamic-slice_fusion.2, bf16[4096,64]{0,1:T(8,128)(2,1)S(1)} %get-tuple-element.116), kind=kOutput, calls=%fused_computation.5.clone.1 | convolution fusion | flops 1082130432 | bytes 1180160 | tf_op jit(solution)/shard_map/while/body/eval_jaxpr/frb,rk->fbk/dot_general | solution.py:23
  98.0 0.6 dynamic_slice.13
  99.2 0.9 constant_dynamic-slice_fusion.2
  100.1 7.5 %fusion.19 = f32[16,8,256,64]{2,3,1,0:T(8,128)} fusion(f32[16,8,256,64]{2,3,1,0:T(8,128)} %get-tuple-element.104, s32[]{:T(128)} %get-tuple-element.103, s32[8,4096]{1,0:T(8,128)S(1)} %constant_dynamic-slice_fusion.2, bf16[4096,64]{0,1:T(8,128)(2,1)S(1)} %get-tuple-element.116), kind=kOutput, calls=%fused_computation.5.clone.1 | convolution fusion | flops 1082130432 | bytes 1180160 | tf_op jit(solution)/shard_map/while/body/eval_jaxpr/frb,rk->fbk/dot_general | solution.py:23
  107.7 0.6 dynamic_slice.13
  108.9 0.9 constant_dynamic-slice_fusion.2
  109.8 7.6 %fusion.19 = f32[16,8,256,64]{2,3,1,0:T(8,128)} fusion(f32[16,8,256,64]{2,3,1,0:T(8,128)} %get-tuple-element.104, s32[]{:T(128)} %get-tuple-element.103, s32[8,4096]{1,0:T(8,128)S(1)} %constant_dynamic-slice_fusion.2, bf16[4096,64]{0,1:T(8,128)(2,1)S(1)} %get-tuple-element.116), kind=kOutput, calls=%fused_computation.5.clone.1 | convolution fusion | flops 1082130432 | bytes 1180160 | tf_op jit(solution)/shard_map/while/body/eval_jaxpr/frb,rk->fbk/dot_general | solution.py:23
  117.4 0.6 dynamic_slice.13
  118.6 0.9 constant_dynamic-slice_fusion.2
  119.5 7.5 %fusion.19 = f32[16,8,256,64]{2,3,1,0:T(8,128)} fusion(f32[16,8,256,64]{2,3,1,0:T(8,128)} %get-tuple-element.104, s32[]{:T(128)} %get-tuple-element.103, s32[8,4096]{1,0:T(8,128)S(1)} %constant_dynamic-slice_fusion.2, bf16[4096,64]{0,1:T(8,128)(2,1)S(1)} %get-tuple-element.116), kind=kOutput, calls=%fused_computation.5.clone.1 | convolution fusion | flops 1082130432 | bytes 1180160 | tf_op jit(solution)/shard_map/while/body/eval_jaxpr/frb,rk->fbk/dot_general | solution.py:23
  127.1 0.6 dynamic_slice.13
  128.3 0.9 constant_dynamic-slice_fusion.2
  129.2 7.5 %fusion.19 = f32[16,8,256,64]{2,3,1,0:T(8,128)} fusion(f32[16,8,256,64]{2,3,1,0:T(8,128)} %get-tuple-element.104, s32[]{:T(128)} %get-tuple-element.103, s32[8,4096]{1,0:T(8,128)S(1)} %constant_dynamic-slice_fusion.2, bf16[4096,64]{0,1:T(8,128)(2,1)S(1)} %get-tuple-element.116), kind=kOutput, calls=%fused_computation.5.clone.1 | convolution fusion | flops 1082130432 | bytes 1180160 | tf_op jit(solution)/shard_map/while/body/eval_jaxpr/frb,rk->fbk/dot_general | solution.py:23
  136.8 0.6 dynamic_slice.13
  138.0 0.9 constant_dynamic-slice_fusion.2
  139.0 7.6 %fusion.19 = f32[16,8,256,64]{2,3,1,0:T(8,128)} fusion(f32[16,8,256,64]{2,3,1,0:T(8,128)} %get-tuple-element.104, s32[]{:T(128)} %get-tuple-element.103, s32[8,4096]{1,0:T(8,128)S(1)} %constant_dynamic-slice_fusion.2, bf16[4096,64]{0,1:T(8,128)(2,1)S(1)} %get-tuple-element.116), kind=kOutput, calls=%fused_computation.5.clone.1 | convolution fusion | flops 1082130432 | bytes 1180160 | tf_op jit(solution)/shard_map/while/body/eval_jaxpr/frb,rk->fbk/dot_general | solution.py:23
  146.5 0.6 dynamic_slice.13
  147.7 0.9 constant_dynamic-slice_fusion.2
  148.7 7.5 %fusion.19 = f32[16,8,256,64]{2,3,1,0:T(8,128)} fusion(f32[16,8,256,64]{2,3,1,0:T(8,128)} %get-tuple-element.104, s32[]{:T(128)} %get-tuple-element.103, s32[8,4096]{1,0:T(8,128)S(1)} %constant_dynamic-slice_fusion.2, bf16[4096,64]{0,1:T(8,128)(2,1)S(1)} %get-tuple-element.116), kind=kOutput, calls=%fused_computation.5.clone.1 | convolution fusion | flops 1082130432 | bytes 1180160 | tf_op jit(solution)/shard_map/while/body/eval_jaxpr/frb,rk->fbk/dot_general | solution.py:23
  156.2 0.6 dynamic_slice.13
  157.5 0.9 constant_dynamic-slice_fusion.2
  158.4 7.6 %fusion.19 = f32[16,8,256,64]{2,3,1,0:T(8,128)} fusion(f32[16,8,256,64]{2,3,1,0:T(8,128)} %get-tuple-element.104, s32[]{:T(128)} %get-tuple-element.103, s32[8,4096]{1,0:T(8,128)S(1)} %constant_dynamic-slice_fusion.2, bf16[4096,64]{0,1:T(8,128)(2,1)S(1)} %get-tuple-element.116), kind=kOutput, calls=%fused_computation.5.clone.1 | convolution fusion | flops 1082130432 | bytes 1180160 | tf_op jit(solution)/shard_map/while/body/eval_jaxpr/frb,rk->fbk/dot_general | solution.py:23
  166.0 0.7 copy-done
  166.7 0.3 fusion.7
  167.0 13.5 %psum.7 = f32[32,2]{0,1:T(2,128)S(1)} all-reduce(f32[32,2]{0,1:T(2,128)S(1)} %fusion.7), channel_id=1, replica_groups=mesh['groups'=2,'dp'=4,'feat'=2,'node'=2] {'dp'}, use_global_device_ids=true, to_apply=%region_5.6 | all-reduce | flops 64 | bytes 512 | tf_op jit(solution)/shard_map/psum | solution.py:52
  180.5 132.8 %reduce-scatter.2.cloned.1.call-done = f32[32,256,64]{1,2,0:T(8,128)} async-done(((f32[128,256,64]{1,2,0:T(8,128)}), f32[32,256,64]{1,2,0:T(8,128)}) %reduce-scatter.2.cloned.1.call-update) | async-done | bytes 2097168 | tf_op jit(solution)/shard_map/reduce_scatter | solution.py:40
  313.3 2.8 copy.12
  316.1 1.6 copy.23
  317.7 64.4 %reduce-window.6 = f32[32,32,2,2,128]{4,1,2,3,0:T(8,128)S(1)} reduce-window(f32[32,32,2,2,128]{4,1,2,3,0:T(8,128)} %bitcast.55, f32[]{:T(128)} %constant.19.clone.1), window={size=1x1x1x1x128 pad=0_0x0_0x0_0x0_0x127_0}, to_apply=%region_3.4 | reduce-window | flops 66584576 | bytes 4194308 | tf_op jit(solution)/shard_map/reduce-window
  382.1 2.0 slice.24
  384.1 2.4 copy.14
  386.7 0.7 bitcast_bitcast_fusion
  387.4 1.6 fusion.15
  389.0 21.6 %pmax.7 = f32[32]{0:T(128)} all-reduce(f32[32]{0:T(128)S(1)} %get-tuple-element.57), channel_id=1, replica_groups=mesh['groups'=2,'dp'=4,'feat'=2,'node'=2] {'dp','feat'}, use_global_device_ids=true, to_apply=%region_7.8 | all-reduce | flops 32 | bytes 256 | tf_op jit(solution)/shard_map/pmax | solution.py:63
  (17 shorter events, 0.3 us)
Async XLA Ops:
  7.2 306.1 %reduce-scatter.2.cloned.1.call-start = ((), (), s32[]{:S(2)}) async-start(), calls=%async_computation.1 | async-start | bytes 10485760 | tf_op jit(solution)/shard_map/reduce_scatter | solution.py:40
  165.9 0.7 copy-start
  165.9 0.7 copy-start.1
  165.9 0.7 copy-start.2
Sparse Core Ops, SparseCore 0:
  166.1 147.1 reduce-scatter.1
where the time goes:
time: 423 us; the launch traced here: 417 us
  waiting for transfers between devices  133 us (31%)
  matrix products  121 us (29%)
  other arithmetic  69.9 us (17%)
  blocking collectives  35.1 us (8%)
  local copies, waits for them, and re-layouts  33.8 us (8%)
  between operations  14.1 us (3%)
  loops' own time  10.6 us (3%)
    reduce_scatter x1, waiting for transfers between devices, on_device(): lax.psum_scatter(histogram(bins, weights, lax.axis_size('dp') * own_featu...  133 us
    dot_general x16, matrix products, one_block(): jnp.einsum('frb,rk->fbk', onehot, weights, preferred_element_type=jnp.flo...  121 us
    another operation x3, other arithmetic  65.2 us
    pmax x1, blocking collectives, on_device(): best = lax.pmax(jnp.max(gains, axis=(1, 2)), ('dp', 'feat'))  21.6 us
    dynamic_slice x16, local copies, waits for them, and re-layouts, one_block(): lax.dynamic_slice_in_dim(bin_table, position * block_size, block_size, 0)  14.7 us
    psum x1, blocking collectives, on_device(): totals = lax.psum(local_totals, 'dp')  13.5 us
    another operation x1, loops' own time, histogram(): lax.map(one_block, jnp.arange(feature_amount // block_size, dtype=jnp.int...  10.6 us
    dynamic_slice x16, local copies, waits for them, and re-layouts, histogram(): lax.map(one_block, jnp.arange(feature_amount // block_size, dtype=jnp.int...  9.32 us
  transfers between devices with their start and end apart: 1, of which 1 were waited for; matrix products, arithmetic and copies ran while one was open for 0% of the time, Pallas kernels for 0%

commit v1 on v0

v1 whole, which is shorter than its diff:
```python
import functools
import math

import jax
import jax.numpy as jnp
from jax import lax
from jax.experimental import pallas as pl
from jax.experimental.pallas import tpu as pltpu
from jax.sharding import PartitionSpec as P

BINS = 256
NODES = 64
LAMBDA_REG = 1.0
MESH = pl.DeviceIdType.MESH
CHUNK = 512


def flip(index, mask, size):
    result, bit = 0, 1
    while bit < size:
        value = (index // bit) % 2
        result = result + bit * ((1 - value) if mask & bit else value)
        bit *= 2
    return result


def partner(index, step, size):
    if size & (size - 1) == 0:
        return flip(index, step, size)
    return (step - index + size) % size


def kernel(
    sizes, bins_ref, aux_ref, gains_ref, best_ref,
    recv, aux, weights, left, ready, row, rows_dp, rows_all,
    local_sem, send_bins, recv_bins, send_aux, recv_aux,
    out_sem, send_out, recv_out, send_dp, recv_dp, send_all, recv_all,
):
    dp, feat, node = sizes
    half, row_count = recv.shape[1:]
    node_count = NODES // node
    z, x, c = lax.axis_index("dp"), lax.axis_index("feat"), lax.axis_index("node")
    group = math.gcd(half, 4)
    others = [(i, k) for i in range(feat) for k in range(node) if (i, k) != (0, 0)]

    def place(i, k):
        return {"feat": (x + i) % feat, "node": (c + k) % node}

    own_bins = pltpu.make_async_copy(bins_ref.at[z, c], recv.at[0], local_sem.at[0])
    own_aux = pltpu.make_async_copy(aux_ref, aux.at[0], local_sem.at[1])
    own_aux.start()
    own_bins.start()

    barrier = pltpu.get_barrier_semaphore()
    for step in range(1, dp):
        pl.semaphore_signal(
            barrier, inc=1, device_id={"dp": partner(z, step, dp)}, device_id_type=MESH
        )
    for i, k in others:
        pl.semaphore_signal(barrier, inc=1, device_id=place(i, k), device_id_type=MESH)
    pl.semaphore_wait(barrier, dp - 1 + len(others))

    copies = []
    for step in range(1, dp):
        to = partner(z, step, dp)
        for source, target, sent, received in (
            (aux_ref, aux, send_aux, recv_aux),
            (bins_ref.at[to, c], recv, send_bins, recv_bins),
        ):
            copy = pltpu.make_async_remote_copy(
                src_ref=source,
                dst_ref=target.at[step],
                send_sem=sent.at[step],
                recv_sem=received.at[step],
                device_id={"dp": to},
                device_id_type=MESH,
            )
            copy.start()
            copies.append(copy)

    ids = lax.broadcasted_iota(jnp.int32, (NODES, CHUNK), 0) + c * node_count
    ids = jnp.where(ids >= NODES, ids - NODES, ids).astype(jnp.float32)
    levels = lax.broadcasted_iota(jnp.int32, (BINS, CHUNK), 0).astype(jnp.float32)
    levels = levels.astype(jnp.bfloat16)

    def one_shard(step, first):
        @pl.loop(0, row_count // CHUNK)
        def _(block):
            span = pl.ds(pl.multiple_of(block * CHUNK, CHUNK), CHUNK)
            mine = aux[step, 0:1, span] == ids
            grad = jnp.where(mine, aux[step, 1:2, span], 0.0)
            hess = jnp.where(mine, aux[step, 2:3, span], 0.0)
            weights[span, :] = jnp.concatenate([grad, hess], 0).astype(jnp.bfloat16).T

        @pl.loop(0, half // group)
        def _(part):
            total = None
            for block in range(row_count // CHUNK):
                span = pl.ds(block * CHUNK, CHUNK)
                pieces = []
                for u in range(group):
                    values = recv[step, pl.ds(part * group + u, 1), span]
                    values = values.astype(jnp.float32).astype(jnp.bfloat16)
                    below = jnp.broadcast_to(values, (BINS, CHUNK)) <= levels
                    pieces.append(jnp.where(below, jnp.bfloat16(1), jnp.bfloat16(0)))
                product = jnp.dot(
                    jnp.concatenate(pieces, 0), weights[span, :], preferred_element_type=jnp.float32
                )
                total = product if total is None else total + product
            sums = total.reshape(group, BINS, 2 * NODES)
            where = pl.ds(part * group, group)
            if first:
                left[where] = sums
            else:
                left[where] += sums

    own_aux.wait()
    own_bins.wait()
    one_shard(0, True)

    @pl.loop(1, dp)
    def _(step):
        for source, target, received in (
            (aux_ref, aux, recv_aux),
            (bins_ref.at[0, 0], recv, recv_bins),
        ):
            pltpu.make_async_copy(source, target.at[step], received.at[step]).wait()
        one_shard(step, False)

    def one_feature(index, largest):
        table = left[index].T
        grad_left, hess_left = table[:NODES], table[NODES:]
        grad_total = grad_left[:, BINS - 1 :]
        hess_total = hess_left[:, BINS - 1 :]
        grad_right = grad_total - grad_left
        gains = 0.5 * (
            grad_left * grad_left / (hess_left + LAMBDA_REG)
            + grad_right * grad_right / (hess_total - hess_left + LAMBDA_REG)
            - grad_total * grad_total / (hess_total + LAMBDA_REG)
        )
        ready[:, pl.ds(index, 1), :] = gains.reshape(NODES, 1, BINS)
        return jnp.maximum(largest, jnp.maximum(gains[:, :128], gains[:, 128:]))

    largest = jnp.full((NODES, 128), -jnp.inf, jnp.float32)
    largest = lax.fori_loop(0, half, one_feature, largest)

    own_out = pltpu.make_async_copy(
        ready.at[pl.ds(0, node_count)], gains_ref.at[:, c], out_sem.at[0]
    )
    own_out.start()
    for k in range(1, node):
        copy = pltpu.make_async_remote_copy(
            src_ref=ready.at[pl.ds(k * node_count, node_count)],
            dst_ref=gains_ref.at[:, c],
            send_sem=send_out.at[k],
            recv_sem=recv_out.at[k],
            device_id={"node": (c + k) % node},
            device_id_type=MESH,
        )
        copy.start()
        copies.append(copy)

    best = jnp.max(largest.T, axis=0, keepdims=True)
    row[0, :, 0:NODES] = jnp.broadcast_to(best, (8, NODES))
    row[0, :, NODES:] = jnp.zeros((8, 128 - NODES), jnp.float32)
    sends = []
    for step in range(1, dp):
        copy = pltpu.make_async_remote_copy(
            src_ref=row.at[0],
            dst_ref=rows_dp.at[step],
            send_sem=send_dp.at[step],
            recv_sem=recv_dp.at[step],
            device_id={"dp": partner(z, step, dp)},
            device_id_type=MESH,
        )
        copy.start()
        sends.append(copy)
    best = row[0]
    for step in range(1, dp):
        sends[step - 1].wait_recv()
        best = jnp.maximum(best, rows_dp[step])
    row[1] = best
    last = []
    for number, (i, k) in enumerate(others):
        copy = pltpu.make_async_remote_copy(
            src_ref=row.at[1],
            dst_ref=rows_all.at[number],
            send_sem=send_all.at[number],
            recv_sem=recv_all.at[number],
            device_id=place(i, k),
            device_id_type=MESH,
        )
        copy.start()
        last.append(copy)
    best = best[:, :node_count]
    for number, (i, k) in enumerate(others):
        last[number].wait_recv()
        best = jnp.maximum(
            best, rows_all[number][:, k * node_count : (k + 1) * node_count]
        )
    best_ref[...] = best

    for copy in copies + sends + last:
        copy.wait_send()
    own_out.wait()
    for k in range(1, node):
        pltpu.make_async_copy(
            ready.at[pl.ds(0, node_count)], gains_ref.at[:, (c + node - k) % node], recv_out.at[k]
        ).wait()


def on_device(sizes, bins, node_ids, grad, hess):
    dp, feat, node = sizes
    feature_block, row_count = bins.shape
    half = feature_block // (dp * node)
    node_count = NODES // node
    aux = jnp.stack(
        [node_ids.astype(jnp.float32), grad.astype(jnp.float32), hess.astype(jnp.float32)], 0
    )
    split = bins.reshape(dp, node, half, row_count)
    peers = max(feat * node - 1, 1)
    dma = pltpu.SemaphoreType.DMA
    gains, best = pl.pallas_call(
        functools.partial(kernel, sizes),
        out_shape=(
            jax.ShapeDtypeStruct((node_count, node, half, BINS), jnp.float32),
            jax.ShapeDtypeStruct((8, node_count), jnp.float32),
        ),
        in_specs=[pl.BlockSpec(memory_space=pl.ANY)] * 2,
        out_specs=(
            pl.BlockSpec(memory_space=pl.ANY),
            pl.BlockSpec(memory_space=pltpu.VMEM),
        ),
        scratch_shapes=[
            pltpu.VMEM((dp, half, row_count), jnp.int32),
            pltpu.VMEM((dp, 3, row_count), jnp.float32),
            pltpu.VMEM((row_count, 2 * NODES), jnp.bfloat16),
            pltpu.VMEM((half, BINS, 2 * NODES), jnp.float32),
            pltpu.VMEM((NODES, half, BINS), jnp.float32),
            pltpu.VMEM((2, 8, 128), jnp.float32),
            pltpu.VMEM((dp, 8, 128), jnp.float32),
            pltpu.VMEM((peers, 8, 128), jnp.float32),
            dma((2,)),
            dma((dp,)), dma((dp,)), dma((dp,)), dma((dp,)),
            dma((1,)), dma((node,)), dma((node,)),
            dma((dp,)), dma((dp,)), dma((peers,)), dma((peers,)),
        ],
        compiler_params=pltpu.CompilerParams(
            collective_id=0, has_side_effects=True, vmem_limit_bytes=40 * 2**20
        ),
        name="split_gains",
    )(split, aux)
    return gains.reshape(node_count, node * half, BINS), best[0]


def solution(mesh):
    sizes = tuple(mesh.shape[axis] for axis in ("dp", "feat", "node"))
    return jax.shard_map(
        functools.partial(on_device, sizes),
        mesh=mesh,
        in_specs=(
            P("feat", ("groups", "dp")),
            P(("groups", "dp")),
            P(("groups", "dp")),
            P(("groups", "dp")),
        ),
        out_specs=(P(("groups", "node"), ("feat", "dp"), None), P(("groups", "node"))),
        check_vma=False,
    )
```

time: 423 us -> 67 us (0.16); the launches traced: 417 us -> 66.6 us
  waiting for transfers between devices: 133 us -> 0 us
  matrix products: 121 us -> 0 us
  other arithmetic: 69.9 us -> 2.17 us
  Pallas kernels: 0 us -> 60.7 us
  blocking collectives: 35.1 us -> 0 us
  local copies, waits for them, and re-layouts: 33.8 us -> 3.07 us
  between operations: 14.1 us -> 0.65 us
  loops' own time: 10.6 us -> 0 us
    reduce_scatter x1 -> x0, waiting for transfers between devices: 133 us -> none  [on_device(): lax.psum_scatter(histogram(bins, weights, lax.axis_size('dp') * own_featu...]
    dot_general x17 -> x0, matrix products: 121 us -> none  [the longest x16 121 us: one_block(): jnp.einsum('frb,rk->fbk', onehot, weights, preferred_element_type=jnp.flo...]
    another operation x4 -> x3, other arithmetic: 66.4 us -> 1.45 us  [on_device(): jnp.stack([node_ids.astype(jnp.float32), grad.astype(jnp.float32), hess.a...]
    pallas_call x0 -> x1, Pallas kernels: none -> 60.7 us  [on_device(): pl.pallas_call(functools.partial(kernel, sizes), out_shape=(jax.ShapeDtyp...]
    dynamic_slice x32 -> x0, local copies, waits for them, and re-layouts: 24 us -> none  [the longest x16 14.7 us: one_block(): lax.dynamic_slice_in_dim(bin_table, position * block_size, block_size, 0)]
    pmax x1 -> x0, blocking collectives: 21.6 us -> none  [on_device(): best = lax.pmax(jnp.max(gains, axis=(1, 2)), ('dp', 'feat'))]
    psum x1 -> x0, blocking collectives: 13.5 us -> none  [on_device(): totals = lax.psum(local_totals, 'dp')]
    another operation x1 -> x0, loops' own time: 10.6 us -> none  [histogram(): lax.map(one_block, jnp.arange(feature_amount // block_size, dtype=jnp.int...]
  transfers between devices with their start and end apart: 1 -> 0, of which waited for: 1 -> 0; matrix products, arithmetic and copies ran while one was open for 0% -> 0% of each run, Pallas kernels for 0% -> 0%
where the time goes in v1:
time: 67 us; the launch traced here: 66.6 us
  Pallas kernels  60.7 us (91%)
  local copies, waits for them, and re-layouts  3.07 us (5%)
  other arithmetic  2.17 us (3%)
    pallas_call x1, Pallas kernels, on_device(): pl.pallas_call(functools.partial(kernel, sizes), out_shape=(jax.ShapeDtyp...  60.7 us
    unnamed x3, local copies, waits for them, and re-layouts  2.56 us
    another operation x3, other arithmetic, on_device(): jnp.stack([node_ids.astype(jnp.float32), grad.astype(jnp.float32), hess.a...  1.45 us

profile of v1, /device:TPU:0, one launch (start us, length us, event | category | flops | bytes accessed | tf_op | source)
XLA Modules:
  0.0 66.6 jit_solution(8906603759580125522)
XLA Ops:
  0.6 0.7 %convert_element_type.2 = f32[4096]{0:T(1024)S(1)} convert(s32[4096]{0:T(1024)} %param.5) | non-fusion elementwise | flops 4096 | bytes 32768 | tf_op jit(solution)/shard_map/convert_element_type | solution.py:218
  1.4 0.7 %stack.24 = f32[4096]{0:T(1024)S(1)} convert(bf16[4096]{0:T(1024)(128)(2,1)} %param.6) | non-fusion elementwise | flops 4096 | bytes 24576 | tf_op jit(solution)/shard_map/stack | solution.py:217
  2.0 0.7 %stack.25 = f32[4096]{0:T(1024)S(1)} convert(bf16[4096]{0:T(1024)(128)(2,1)} %param.7) | non-fusion elementwise | flops 4096 | bytes 24576 | tf_op jit(solution)/shard_map/stack | solution.py:217
  2.8 0.0 copy-start
  2.8 1.6 %copy-done = s32[128,4096]{1,0:T(8,128)S(1)} copy-done((s32[128,4096]{1,0:T(8,128)S(1)}, s32[128,4096]{1,0:T(8,128)}, u32[]{:S(2)}) %copy-start) | copy-done | bytes 2097176
  4.4 60.7 %split_gains.1 = (f32[32,2,16,256]{3,2,1,0:T(8,128)S(1)}, f32[8,32]{1,0:T(8,128)S(1)}) custom-call(s32[4,2,16,4096]{3,2,1,0:T(8,128)S(1)} %bitcast.7, f32[3,4096]{1,0:T(4,128)S(1)} %pad_maximum_fusion.aux_ref), custom_call_target="tpu_custom_call" | custom-call | tf_op jit(solution)/shard_map/split_gains/pallas_call | solution.py:223
  65.1 0.5 slice_bitcast_fusion
  65.6 1.0 %copy.7 = f32[32,32,256]{2,1,0:T(8,128)} copy(f32[32,32,256]{2,1,0:T(8,128)S(1)} %bitcast.8) | data formatting | bytes 2097152
  (1 shorter events, 0.0 us)
Async XLA Ops:
  2.8 1.6 %copy-start = (s32[128,4096]{1,0:T(8,128)S(1)}, s32[128,4096]{1,0:T(8,128)}, u32[]{:S(2)}) copy-start(s32[128,4096]{1,0:T(8,128)} %param.4) | copy-start | bytes 6291460

commit v2 on v1

--- a/solution.py
+++ b/solution.py
@@ -41,6 +41,7 @@
     node_count = NODES // node
     z, x, c = lax.axis_index("dp"), lax.axis_index("feat"), lax.axis_index("node")
     group = math.gcd(half, 4)
+    parts = half // group
     others = [(i, k) for i in range(feat) for k in range(node) if (i, k) != (0, 0)]
 
     def place(i, k):
@@ -58,6 +59,21 @@
         )
     for i, k in others:
         pl.semaphore_signal(barrier, inc=1, device_id=place(i, k), device_id_type=MESH)
+    ids = lax.broadcasted_iota(jnp.int32, (NODES, CHUNK), 0) + c * node_count
+    ids = jnp.where(ids >= NODES, ids - NODES, ids).astype(jnp.float32)
+    levels = lax.broadcasted_iota(jnp.int32, (BINS, CHUNK), 0).astype(jnp.float32)
+    levels = levels.astype(jnp.bfloat16)
+
+    def build(step):
+        for block in range(row_count // CHUNK):
+            span = pl.ds(block * CHUNK, CHUNK)
+            mine = aux[step, 0:1, span] == ids
+            grad = jnp.where(mine, aux[step, 1:2, span], 0.0)
+            hess = jnp.where(mine, aux[step, 2:3, span], 0.0)
+            weights[span, :] = jnp.concatenate([grad, hess], 0).astype(jnp.bfloat16).T
+
+    own_aux.wait()
+    build(0)
     pl.semaphore_wait(barrier, dp - 1 + len(others))
 
     copies = []
@@ -78,54 +94,48 @@
             copy.start()
             copies.append(copy)
 
-    ids = lax.broadcasted_iota(jnp.int32, (NODES, CHUNK), 0) + c * node_count
-    ids = jnp.where(ids >= NODES, ids - NODES, ids).astype(jnp.float32)
-    levels = lax.broadcasted_iota(jnp.int32, (BINS, CHUNK), 0).astype(jnp.float32)
-    levels = levels.astype(jnp.bfloat16)
-
-    def one_shard(step, first):
-        @pl.loop(0, row_count // CHUNK)
-        def _(block):
-            span = pl.ds(pl.multiple_of(block * CHUNK, CHUNK), CHUNK)
-            mine = aux[step, 0:1, span] == ids
-            grad = jnp.where(mine, aux[step, 1:2, span], 0.0)
-            hess = jnp.where(mine, aux[step, 2:3, span], 0.0)
-            weights[span, :] = jnp.concatenate([grad, hess], 0).astype(jnp.bfloat16).T
-
-        @pl.loop(0, half // group)
-        def _(part):
-            total = None
-            for block in range(row_count // CHUNK):
-                span = pl.ds(block * CHUNK, CHUNK)
-                pieces = []
-                for u in range(group):
-                    values = recv[step, pl.ds(part * group + u, 1), span]
-                    values = values.astype(jnp.float32).astype(jnp.bfloat16)
-                    below = jnp.broadcast_to(values, (BINS, CHUNK)) <= levels
-                    pieces.append(jnp.where(below, jnp.bfloat16(1), jnp.bfloat16(0)))
-                product = jnp.dot(
-                    jnp.concatenate(pieces, 0), weights[span, :], preferred_element_type=jnp.float32
-                )
-                total = product if total is None else total + product
-            sums = total.reshape(group, BINS, 2 * NODES)
-            where = pl.ds(part * group, group)
-            if first:
-                left[where] = sums
-            else:
-                left[where] += sums
-
-    own_aux.wait()
+    def add_rows(step, part, first):
+        total = None
+        for block in range(row_count // CHUNK):
+            span = pl.ds(block * CHUNK, CHUNK)
+            pieces = []
+            for u in range(group):
+                values = recv[step, pl.ds(part * group + u, 1), span]
+                values = values.astype(jnp.float32).astype(jnp.bfloat16)
+                below = jnp.broadcast_to(values, (BINS, CHUNK)) <= levels
+                pieces.append(jnp.where(below, jnp.bfloat16(1), jnp.bfloat16(0)))
+            product = jnp.dot(
+                jnp.concatenate(pieces, 0), weights[span, :], preferred_element_type=jnp.float32
+            )
+            total = product if total is None else total + product
+        sums = total.reshape(group, BINS, 2 * NODES)
+        where = pl.ds(part * group, group)
+        if first:
+            left[where] = sums
+        else:
+            left[where] += sums
+
     own_bins.wait()
-    one_shard(0, True)
-
-    @pl.loop(1, dp)
-    def _(step):
+
+    @pl.loop(0, parts)
+    def _(part):
+        add_rows(0, part, True)
+
+    def arrive(step):
         for source, target, received in (
             (aux_ref, aux, recv_aux),
             (bins_ref.at[0, 0], recv, recv_bins),
         ):
             pltpu.make_async_copy(source, target.at[step], received.at[step]).wait()
-        one_shard(step, False)
+        build(step)
+
+    @pl.loop(1, dp - 1)
+    def _(step):
+        arrive(step)
+
+        @pl.loop(0, parts)
+        def _(part):
+            add_rows(step, part, False)
 
     def one_feature(index, largest):
         table = left[index].T
@@ -141,24 +151,45 @@
         ready[:, pl.ds(index, 1), :] = gains.reshape(NODES, 1, BINS)
         return jnp.maximum(largest, jnp.maximum(gains[:, :128], gains[:, 128:]))
 
+    def finish(part, largest):
+        for u in range(group):
+            largest = one_feature(part * group + u, largest)
+        return largest
+
+    def finish_and_add(part, largest):
+        largest = finish(part - 1, largest)
+        add_rows(dp - 1, part, False)
+        return largest
+
+    def hand_out(number, start, size):
+        span = pl.ds(start, size)
+        copy = pltpu.make_async_copy(
+            ready.at[pl.ds(0, node_count), span], gains_ref.at[:, c, span], out_sem.at[number]
+        )
+        copy.start()
+        outs.append(copy)
+        for k in range(1, node):
+            copy = pltpu.make_async_remote_copy(
+                src_ref=ready.at[pl.ds(k * node_count, node_count), span],
+                dst_ref=gains_ref.at[:, c, span],
+                send_sem=send_out.at[number, k],
+                recv_sem=recv_out.at[number, k],
+                device_id={"node": (c + k) % node},
+                device_id_type=MESH,
+            )
+            copy.start()
+            copies.append(copy)
+
+    outs = []
+    early = (half - group) // 8 * 8
     largest = jnp.full((NODES, 128), -jnp.inf, jnp.float32)
-    largest = lax.fori_loop(0, half, one_feature, largest)
-
-    own_out = pltpu.make_async_copy(
-        ready.at[pl.ds(0, node_count)], gains_ref.at[:, c], out_sem.at[0]
-    )
-    own_out.start()
-    for k in range(1, node):
-        copy = pltpu.make_async_remote_copy(
-            src_ref=ready.at[pl.ds(k * node_count, node_count)],
-            dst_ref=gains_ref.at[:, c],
-            send_sem=send_out.at[k],
-            recv_sem=recv_out.at[k],
-            device_id={"node": (c + k) % node},
-            device_id_type=MESH,
-        )
-        copy.start()
-        copies.append(copy)
+    arrive(dp - 1)
+    add_rows(dp - 1, 0, False)
+    largest = lax.fori_loop(1, parts, finish_and_add, largest)
+    if early:
+        hand_out(0, 0, early)
+    largest = finish(parts - 1, largest)
+    hand_out(1, early, half - early)
 
     best = jnp.max(largest.T, axis=0, keepdims=True)
     row[0, :, 0:NODES] = jnp.broadcast_to(best, (8, NODES))
@@ -202,11 +233,17 @@
 
     for copy in copies + sends + last:
         copy.wait_send()
-    own_out.wait()
-    for k in range(1, node):
-        pltpu.make_async_copy(
-            ready.at[pl.ds(0, node_count)], gains_ref.at[:, (c + node - k) % node], recv_out.at[k]
-        ).wait()
+    for copy in outs:
+        copy.wait()
+    for number, start, size in ((0, 0, early), (1, early, half - early)):
+        for k in range(1, node):
+            if size:
+                span = pl.ds(start, size)
+                pltpu.make_async_copy(
+                    ready.at[pl.ds(0, node_count), span],
+                    gains_ref.at[:, (c + node - k) % node, span],
+                    recv_out.at[number, k],
+                ).wait()
 
 
 def on_device(sizes, bins, node_ids, grad, hess):
@@ -214,8 +251,11 @@
     feature_block, row_count = bins.shape
     half = feature_block // (dp * node)
     node_count = NODES // node
-    aux = jnp.stack(
-        [node_ids.astype(jnp.float32), grad.astype(jnp.float32), hess.astype(jnp.float32)], 0
+    line = lax.broadcasted_iota(jnp.int32, (3, row_count), 0)
+    aux = jnp.where(
+        line == 0,
+        node_ids.astype(jnp.float32)[None],
+        jnp.where(line == 1, grad.astype(jnp.float32)[None], hess.astype(jnp.float32)[None]),
     )
     split = bins.reshape(dp, node, half, row_count)
     peers = max(feat * node - 1, 1)
@@ -226,7 +266,7 @@
             jax.ShapeDtypeStruct((node_count, node, half, BINS), jnp.float32),
             jax.ShapeDtypeStruct((8, node_count), jnp.float32),
         ),
-        in_specs=[pl.BlockSpec(memory_space=pl.ANY)] * 2,
+        in_specs=[pl.BlockSpec(memory_space=pltpu.HBM), pl.BlockSpec(memory_space=pl.ANY)],
         out_specs=(
             pl.BlockSpec(memory_space=pl.ANY),
             pl.BlockSpec(memory_space=pltpu.VMEM),
@@ -242,11 +282,11 @@
             pltpu.VMEM((peers, 8, 128), jnp.float32),
             dma((2,)),
             dma((dp,)), dma((dp,)), dma((dp,)), dma((dp,)),
-            dma((1,)), dma((node,)), dma((node,)),
+            dma((2,)), dma((2, node)), dma((2, node)),
             dma((dp,)), dma((dp,)), dma((peers,)), dma((peers,)),
         ],
         compiler_params=pltpu.CompilerParams(
-            collective_id=0, has_side_effects=True, vmem_limit_bytes=40 * 2**20
+            collective_id=0, has_side_effects=True, vmem_limit_bytes=56 * 2**20
         ),
         name="split_gains",
     )(split, aux)

time: 67 us -> 64.9 us (0.969)
  Pallas kernels: 60.7 us -> 57.6 us
    pallas_call x1, Pallas kernels: 60.7 us -> 57.6 us  [on_device(): pl.pallas_call(functools.partial(kernel, sizes), out_shape=(jax.ShapeDtyp...]
    another operation x3 -> x0, other arithmetic: 1.45 us -> none  [on_device(): jnp.stack([node_ids.astype(jnp.float32), grad.astype(jnp.float32), hess.a...]
    convert_element_type x1 -> x3, other arithmetic: 0.72 us -> 2.12 us  [the longest x1 0.72 us: on_device(): node_ids.astype(jnp.float32)[None]]
    select_n x0 -> x1, other arithmetic: none -> 0.71 us  [on_device(): jnp.where(line == 0, node_ids.astype(jnp.float32)[None], jnp.where(line =...]
    squeeze x1, local copies, waits for them, and re-layouts: 0.51 us -> 1.18 us  [on_device(): return (gains.reshape(node_count, node * half, BINS), best[0])]
    unnamed x3 -> x1, local copies, waits for them, and re-layouts: 2.56 us -> 2.31 us
where the time goes in v2:
time: 64.9 us; the launch traced here: 64.5 us
  Pallas kernels  57.6 us (89%)
  local copies, waits for them, and re-layouts  3.49 us (5%)
  other arithmetic  2.84 us (4%)
  between operations  0.65 us (1%)
    pallas_call x1, Pallas kernels, on_device(): pl.pallas_call(functools.partial(kernel, sizes), out_shape=(jax.ShapeDtyp...  57.6 us
    unnamed x1, local copies, waits for them, and re-layouts  2.31 us

profile of v2, /device:TPU:0, one launch (start us, length us, event | category | flops | bytes accessed | tf_op | source)
XLA Modules:
  0.0 64.5 jit_solution(14171255254811101935)
XLA Ops:
  0.6 0.7 %convert_element_type.9 = f32[4096]{0:T(1024)S(1)} convert(s32[4096]{0:T(1024)} %param.5) | non-fusion elementwise | flops 4096 | bytes 32768 | tf_op jit(solution)/shard_map/convert_element_type | solution.py:257
  1.4 0.7 %convert_element_type.10 = f32[4096]{0:T(1024)S(1)} convert(bf16[4096]{0:T(1024)(128)(2,1)} %param.6) | non-fusion elementwise | flops 4096 | bytes 24576 | tf_op jit(solution)/shard_map/convert_element_type | solution.py:258
  2.1 0.7 %convert_element_type.11 = f32[4096]{0:T(1024)S(1)} convert(bf16[4096]{0:T(1024)(128)(2,1)} %param.7) | non-fusion elementwise | flops 4096 | bytes 24576 | tf_op jit(solution)/shard_map/convert_element_type | solution.py:258
  2.8 0.7 %select_select_fusion.aux_ref = f32[3,4096]{1,0:T(4,128)} fusion(f32[4096]{0:T(1024)S(1)} %convert_element_type.11, f32[4096]{0:T(1024)S(1)} %convert_element_type.10, f32[4096]{0:T(1024)S(1)} %convert_element_type.9, pred[3]{0:T(512)(128)(4,1)S(1)} %get-tuple-element.6, pred[3]{0:T(512)(128)(4,1)S(1)} %get-tuple-element.7), kind=kLoop, calls=%fused_computation | loop fusion | flops 24576 | bytes 98310 | tf_op jit(solution)/shard_map/jit(_where)/select_n | solution.py:255
  3.5 57.6 %split_gains.1 = (f32[32,2,16,256]{3,2,1,0:T(8,128)}, f32[8,32]{1,0:T(8,128)}) custom-call(s32[4,2,16,4096]{3,2,1,0:T(8,128)} %bitcast.4, f32[3,4096]{1,0:T(4,128)} %select_select_fusion.aux_ref), custom_call_target="tpu_custom_call" | custom-call | tf_op jit(solution)/shard_map/split_gains/pallas_call | solution.py:263
  61.0 1.2 %slice_bitcast_fusion = f32[32]{0:T(128)} fusion(f32[8,32]{1,0:T(8,128)} %get-tuple-element.5), kind=kLoop, calls=%fused_computation.1 | loop fusion | bytes 256 | tf_op jit(solution)/shard_map/squeeze | solution.py:293
  62.2 2.3 %copy.7 = f32[32,32,256]{2,1,0:T(8,128)} copy(f32[32,32,256]{2,1,0:T(8,128)} %bitcast.5) | data formatting | bytes 2097152
  (1 shorter events, 0.0 us)

commit v3 on v2

--- a/solution.py
+++ b/solution.py
@@ -40,7 +40,7 @@
     half, row_count = recv.shape[1:]
     node_count = NODES // node
     z, x, c = lax.axis_index("dp"), lax.axis_index("feat"), lax.axis_index("node")
-    group = math.gcd(half, 4)
+    group = math.gcd(half, 8)
     parts = half // group
     others = [(i, k) for i in range(feat) for k in range(node) if (i, k) != (0, 0)]
 
@@ -72,8 +72,6 @@
             hess = jnp.where(mine, aux[step, 2:3, span], 0.0)
             weights[span, :] = jnp.concatenate([grad, hess], 0).astype(jnp.bfloat16).T
 
-    own_aux.wait()
-    build(0)
     pl.semaphore_wait(barrier, dp - 1 + len(others))
 
     copies = []
@@ -115,6 +113,8 @@
         else:
             left[where] += sums
 
+    own_aux.wait()
+    build(0)
     own_bins.wait()
 
     @pl.loop(0, parts)
@@ -286,7 +286,7 @@
             dma((dp,)), dma((dp,)), dma((peers,)), dma((peers,)),
         ],
         compiler_params=pltpu.CompilerParams(
-            collective_id=0, has_side_effects=True, vmem_limit_bytes=56 * 2**20
+            collective_id=0, has_side_effects=True, vmem_limit_bytes=40 * 2**20
         ),
         name="split_gains",
     )(split, aux)

time: 64.9 us -> 62.2 us (0.958)
  Pallas kernels: 57.6 us -> 55.9 us
    pallas_call x1, Pallas kernels: 57.6 us -> 55.9 us  [on_device(): pl.pallas_call(functools.partial(kernel, sizes), out_shape=(jax.ShapeDtyp...]
    squeeze x1, local copies, waits for them, and re-layouts: 1.18 us -> 0.51 us  [on_device(): return (gains.reshape(node_count, node * half, BINS), best[0])]
    unnamed x1 -> x3, local copies, waits for them, and re-layouts: 2.31 us -> 2.56 us
where the time goes in v3:
time: 62.2 us; the launch traced here: 61.8 us
  Pallas kernels  55.9 us (90%)
  local copies, waits for them, and re-layouts  3.07 us (5%)
  other arithmetic  2.21 us (4%)
  between operations  0.66 us (1%)
    pallas_call x1, Pallas kernels, on_device(): pl.pallas_call(functools.partial(kernel, sizes), out_shape=(jax.ShapeDtyp...  55.9 us
    unnamed x3, local copies, waits for them, and re-layouts  2.56 us

profile of v3, /device:TPU:0, one launch (start us, length us, event | category | flops | bytes accessed | tf_op | source)
XLA Modules:
  0.0 61.8 jit_solution(5641433942215558412)
XLA Ops:
  0.6 0.7 %convert_element_type.9 = f32[4096]{0:T(1024)S(1)} convert(s32[4096]{0:T(1024)} %param.5) | non-fusion elementwise | flops 4096 | bytes 32768 | tf_op jit(solution)/shard_map/convert_element_type | solution.py:257
  1.4 0.7 %convert_element_type.10 = f32[4096]{0:T(1024)S(1)} convert(bf16[4096]{0:T(1024)(128)(2,1)} %param.6) | non-fusion elementwise | flops 4096 | bytes 24576 | tf_op jit(solution)/shard_map/convert_element_type | solution.py:258
  2.1 0.7 %convert_element_type.11 = f32[4096]{0:T(1024)S(1)} convert(bf16[4096]{0:T(1024)(128)(2,1)} %param.7) | non-fusion elementwise | flops 4096 | bytes 24576 | tf_op jit(solution)/shard_map/convert_element_type | solution.py:258
  2.8 0.1 select_select_fusion.aux_ref
  2.9 0.0 copy-start
  2.9 1.6 %copy-done = s32[128,4096]{1,0:T(8,128)S(1)} copy-done((s32[128,4096]{1,0:T(8,128)S(1)}, s32[128,4096]{1,0:T(8,128)}, u32[]{:S(2)}) %copy-start) | copy-done | bytes 2097176
  4.4 55.9 %split_gains.1 = (f32[32,2,16,256]{3,2,1,0:T(8,128)S(1)}, f32[8,32]{1,0:T(8,128)S(1)}) custom-call(s32[4,2,16,4096]{3,2,1,0:T(8,128)S(1)} %bitcast.4, f32[3,4096]{1,0:T(4,128)S(1)} %select_select_fusion.aux_ref), custom_call_target="tpu_custom_call" | custom-call | tf_op jit(solution)/shard_map/split_gains/pallas_call | solution.py:263
  60.3 0.5 slice_bitcast_fusion
  60.8 1.0 %copy.7 = f32[32,32,256]{2,1,0:T(8,128)} copy(f32[32,32,256]{2,1,0:T(8,128)S(1)} %bitcast.5) | data formatting | bytes 2097152
  (1 shorter events, 0.0 us)
Async XLA Ops:
  2.9 1.6 %copy-start = (s32[128,4096]{1,0:T(8,128)S(1)}, s32[128,4096]{1,0:T(8,128)}, u32[]{:S(2)}) copy-start(s32[128,4096]{1,0:T(8,128)} %param.4) | copy-start | bytes 6291460

commit v4 on v3

--- a/solution.py
+++ b/solution.py
@@ -251,11 +251,8 @@
     feature_block, row_count = bins.shape
     half = feature_block // (dp * node)
     node_count = NODES // node
-    line = lax.broadcasted_iota(jnp.int32, (3, row_count), 0)
-    aux = jnp.where(
-        line == 0,
-        node_ids.astype(jnp.float32)[None],
-        jnp.where(line == 1, grad.astype(jnp.float32)[None], hess.astype(jnp.float32)[None]),
+    aux = jnp.stack(
+        [node_ids.astype(jnp.float32), grad.astype(jnp.float32), hess.astype(jnp.float32)], 0
     )
     split = bins.reshape(dp, node, half, row_count)
     peers = max(feat * node - 1, 1)

time: 62.2 us -> 62.1 us (level)
    another operation x0 -> x3, other arithmetic: none -> 1.45 us  [on_device(): jnp.stack([node_ids.astype(jnp.float32), grad.astype(jnp.float32), hess.a...]
    convert_element_type x3 -> x1, other arithmetic: 2.12 us -> 0.72 us  [on_device(): node_ids.astype(jnp.float32)]
where the time goes in v4:
time: 62.1 us; the launch traced here: 61.7 us
  Pallas kernels  55.9 us (90%)
  local copies, waits for them, and re-layouts  3.07 us (5%)
  other arithmetic  2.17 us (3%)
  between operations  0.65 us (1%)
    pallas_call x1, Pallas kernels, on_device(): pl.pallas_call(functools.partial(kernel, sizes), out_shape=(jax.ShapeDtyp...  55.9 us
    unnamed x3, local copies, waits for them, and re-layouts  2.56 us
    another operation x3, other arithmetic, on_device(): jnp.stack([node_ids.astype(jnp.float32), grad.astype(jnp.float32), hess.a...  1.45 us

profile of v4, /device:TPU:0, one launch (start us, length us, event | category | flops | bytes accessed | tf_op | source)
XLA Modules:
  0.0 61.7 jit_solution(9694287345945282214)
XLA Ops:
  0.6 0.7 %convert_element_type.2 = f32[4096]{0:T(1024)S(1)} convert(s32[4096]{0:T(1024)} %param.5) | non-fusion elementwise | flops 4096 | bytes 32768 | tf_op jit(solution)/shard_map/convert_element_type | solution.py:255
  1.4 0.7 %stack.24 = f32[4096]{0:T(1024)S(1)} convert(bf16[4096]{0:T(1024)(128)(2,1)} %param.6) | non-fusion elementwise | flops 4096 | bytes 24576 | tf_op jit(solution)/shard_map/stack | solution.py:254
  2.0 0.7 %stack.25 = f32[4096]{0:T(1024)S(1)} convert(bf16[4096]{0:T(1024)(128)(2,1)} %param.7) | non-fusion elementwise | flops 4096 | bytes 24576 | tf_op jit(solution)/shard_map/stack | solution.py:254
  2.8 0.0 copy-start
  2.8 1.6 %copy-done = s32[128,4096]{1,0:T(8,128)S(1)} copy-done((s32[128,4096]{1,0:T(8,128)S(1)}, s32[128,4096]{1,0:T(8,128)}, u32[]{:S(2)}) %copy-start) | copy-done | bytes 2097176
  4.4 55.9 %split_gains.1 = (f32[32,2,16,256]{3,2,1,0:T(8,128)S(1)}, f32[8,32]{1,0:T(8,128)S(1)}) custom-call(s32[4,2,16,4096]{3,2,1,0:T(8,128)S(1)} %bitcast.7, f32[3,4096]{1,0:T(4,128)S(1)} %pad_maximum_fusion.aux_ref), custom_call_target="tpu_custom_call" | custom-call | tf_op jit(solution)/shard_map/split_gains/pallas_call | solution.py:260
  60.3 0.5 slice_bitcast_fusion
  60.8 1.0 %copy.7 = f32[32,32,256]{2,1,0:T(8,128)} copy(f32[32,32,256]{2,1,0:T(8,128)S(1)} %bitcast.8) | data formatting | bytes 2097152
  (1 shorter events, 0.0 us)
Async XLA Ops:
  2.8 1.6 %copy-start = (s32[128,4096]{1,0:T(8,128)S(1)}, s32[128,4096]{1,0:T(8,128)}, u32[]{:S(2)}) copy-start(s32[128,4096]{1,0:T(8,128)} %param.4) | copy-start | bytes 6291460
